TPU v7x, 256 devices: a whole 4x4x8 slice. The times are simulated.
256 devices in a mesh: row: 16 (over z, core), col: 16 (over y, x).
Axes of the slice: x: 4, y: 4, z: 8, core: 2. Of those that a mesh axis runs over, the one named last changes fastest.
Arguments:
- momentum: float32 [8192, 26624], P('row', 'col'), may hold values from -20 to 20
- grad: bfloat16 [8192, 26624], P('row', 'col'), may hold values from -3 to 3
- basis: float32 [26624, 128], P('col'), may hold values from -0.0390625 to 0.0390625
Outputs:
- momentum_out: float32 [8192, 26624], P('row', 'col')
- left_out: float32 [2, 8192, 128], P(None, 'row')
- right_out: float32 [26624, 128], P('col')
All inputs are finite; a program needn't handle non-finite values.
Results may differ from a plain program's by a relative error of at most 0.0003.
Values sent between devices are 32-bit elements; how exact they have to be, the bound alone decides.
A program may use at most 64 MiB of HBM per device.

v0:
```python
import jax
import jax.numpy as jnp
from jax import lax
from jax.sharding import PartitionSpec as P

ITERS = 2


def chol_solve(share, gram):
    lower = jnp.linalg.cholesky(gram)
    return jax.scipy.linalg.solve_triangular(lower, share.T, lower=True).T


def gram_of(share):
    return lax.dot_general(share, share, (((0,), (0,)), ((), ())), precision=lax.Precision.HIGHEST)


def shards(momentum, grad, basis):
    work = momentum + grad.astype(jnp.float32)
    row_count = momentum.shape[0]
    col_count = momentum.shape[1]
    total_rows = row_count * lax.axis_size("row")
    total_cols = col_count * lax.axis_size("col")
    lefts = []
    for step in range(ITERS):
        current = work
        current_basis = basis
        proj = lax.psum(jnp.dot(current, current_basis, precision=lax.Precision.HIGHEST), "col")
        gram_left = lax.psum(gram_of(proj), "row")
        left = chol_solve(proj, gram_left)
        partial_right = lax.dot_general(
            current, left, (((0,), (0,)), ((), ())), precision=lax.Precision.HIGHEST
        )
        right_raw = lax.psum(partial_right, "row")
        gram_right = lax.psum(gram_of(right_raw), "col")
        basis = chol_solve(right_raw, gram_right)
        outer = lax.dot_general(
            left, right_raw, (((1,), (1,)), ((), ())), precision=lax.Precision.HIGHEST
        )
        work = current - 0.95 * outer
        lefts.append(left * jnp.sqrt(jnp.float32(total_rows)))
    return (work, jnp.stack(lefts), basis * jnp.sqrt(jnp.float32(total_cols)))


def solution(mesh):
    in_specs = (P("row", "col"), P("row", "col"), P("col", None))
    out_specs = (P("row", "col"), P(None, "row", None), P("col", None))
    return jax.shard_map(shards, mesh=mesh, in_specs=in_specs, out_specs=out_specs, check_vma=False)
```

profile of v0, /device:TPU:2, one launch (start us, length us, event | category | flops | bytes accessed | tf_op | source)
XLA Modules:
  0.0 950.0 jit_solution(10892102189534766534)
XLA Ops:
  7.2 0.0 all-reduce.9.cloned.1.call-start
  7.2 1.1 copy-done
  8.3 6.2 fusion.2
  14.5 0.0 all-reduce.9.cloned.1.call-update
  14.5 0.0 all-reduce.11.cloned.1.call-start
  14.6 97.0 %all-reduce.9.cloned.1.call-done = f32[512,128]{1,0:T(8,128)} async-done(((f32[512,128]{1,0:T(8,128)}), f32[512,128]{1,0:T(8,128)}) %all-reduce.9.cloned.1.call-update) | async-done | bytes 262160 | tf_op jit(solution)/shard_map/psum | solution.py:28
  111.6 2.2 fusion.22
  113.8 0.0 all-reduce.11.cloned.1.call-update
  113.8 0.2 all-reduce.13.cloned.1.call-start
  114.1 99.1 %all-reduce.11.cloned.1.call-done = f32[128,128]{0,1:T(8,128)} async-done(((f32[128,128]{0,1:T(8,128)}), f32[128,128]{0,1:T(8,128)}) %all-reduce.11.cloned.1.call-update) | async-done | bytes 65552 | tf_op jit(solution)/shard_map/psum | solution.py:29
  213.1 0.9 copy.7
  214.0 0.9 fusion.21
  214.9 11.7 %cholesky.74 = f32[128,128]{1,0:T(8,128)S(1)} custom-call(f32[128,128]{1,0:T(8,128)S(1)} %fusion.21), custom_call_target="Cholesky" | custom-call | tf_op jit(solution)/shard_map/jit(cholesky)/cholesky | solution.py:10
  226.6 0.6 compare_reduce_fusion.3
  227.3 0.7 fusion.10
  228.0 9.8 %custom-call.10 = f32[1,128,128]{1,2,0:T(8,128)S(1)} custom-call(f32[1,128,128]{2,1,0:T(8,128)S(1)} %fusion.10), custom_call_target="InvertDiagBlocksLowerTriangular" | custom-call | tf_op jit(solution)/shard_map/jit(_solve_triangular)/triangular_solve | solution.py:11
  237.8 1.4 fusion.8
  239.2 0.7 copy-done.4
  239.9 8.3 fusion.1
  248.2 0.0 all-reduce.13.cloned.1.call-update
  248.2 0.0 all-reduce.15.cloned.1.call-start
  248.3 109.5 %all-reduce.13.cloned.1.call-done = f32[1664,128]{1,0:T(8,128)} async-done(((f32[1664,128]{1,0:T(8,128)}), f32[1664,128]{1,0:T(8,128)}) %all-reduce.13.cloned.1.call-update) | async-done | bytes 851984 | tf_op jit(solution)/shard_map/psum | solution.py:34
  357.8 3.5 fusion.23
  361.4 0.4 all-reduce.17.cloned.1.call-start
  361.8 7.3 multiply_subtract_fusion.1
  369.2 82.3 %all-reduce.15.cloned.1.call-done = f32[128,128]{0,1:T(8,128)} async-done(((f32[128,128]{0,1:T(8,128)}), f32[128,128]{0,1:T(8,128)}) %all-reduce.15.cloned.1.call-update) | async-done | bytes 65552 | tf_op jit(solution)/shard_map/psum | solution.py:35
  451.5 0.9 copy.9
  452.4 0.9 fusion.19
  453.3 11.7 %cholesky.85 = f32[128,128]{1,0:T(8,128)S(1)} custom-call(f32[128,128]{1,0:T(8,128)S(1)} %fusion.19), custom_call_target="Cholesky" | custom-call | tf_op jit(solution)/shard_map/jit(cholesky)/cholesky | solution.py:10
  465.0 0.6 compare_reduce_fusion.2
  465.7 0.7 fusion.11
  466.4 9.8 %custom-call.11 = f32[1,128,128]{1,2,0:T(8,128)S(1)} custom-call(f32[1,128,128]{2,1,0:T(8,128)S(1)} %fusion.11), custom_call_target="InvertDiagBlocksLowerTriangular" | custom-call | tf_op jit(solution)/shard_map/jit(_solve_triangular)/triangular_solve | solution.py:11
  476.2 1.0 fusion.4
  477.1 5.8 fusion.24
  482.9 0.0 all-reduce.17.cloned.1.call-update
  482.9 0.0 all-reduce.19.cloned.1.call-start
  483.0 93.9 %all-reduce.17.cloned.1.call-done = f32[512,128]{1,0:T(8,128)} async-done(((f32[512,128]{1,0:T(8,128)}), f32[512,128]{1,0:T(8,128)}) %all-reduce.17.cloned.1.call-update) | async-done | bytes 262160 | tf_op jit(solution)/shard_map/psum | solution.py:28
  576.8 2.2 fusion.25
  579.1 0.0 all-reduce.19.cloned.1.call-update
  579.1 0.0 all-reduce.21.cloned.1.call-start
  579.2 99.1 %all-reduce.19.cloned.1.call-done = f32[128,128]{0,1:T(8,128)} async-done(((f32[128,128]{0,1:T(8,128)}), f32[128,128]{0,1:T(8,128)}) %all-reduce.19.cloned.1.call-update) | async-done | bytes 65552 | tf_op jit(solution)/shard_map/psum | solution.py:29
  678.3 0.9 copy.11
  679.2 0.9 fusion.17
  680.0 11.7 %cholesky.96 = f32[128,128]{1,0:T(8,128)S(1)} custom-call(f32[128,128]{1,0:T(8,128)S(1)} %fusion.17), custom_call_target="Cholesky" | custom-call | tf_op jit(solution)/shard_map/jit(cholesky)/cholesky | solution.py:10
  691.8 0.6 compare_reduce_fusion.1
  692.4 0.7 fusion.12
  693.1 9.8 %custom-call.12 = f32[1,128,128]{1,2,0:T(8,128)S(1)} custom-call(f32[1,128,128]{2,1,0:T(8,128)S(1)} %fusion.12), custom_call_target="InvertDiagBlocksLowerTriangular" | custom-call | tf_op jit(solution)/shard_map/jit(_solve_triangular)/triangular_solve | solution.py:11
  702.9 1.4 fusion.6
  704.3 8.3 fusion.26
  712.7 0.3 all-reduce.23.cloned.1.call-start
  713.0 1.0 copy.14
  714.0 108.2 %all-reduce.21.cloned.1.call-done = f32[1664,128]{1,0:T(8,128)} async-done(((f32[1664,128]{1,0:T(8,128)}), f32[1664,128]{1,0:T(8,128)}) %all-reduce.21.cloned.1.call-update) | async-done | bytes 851984 | tf_op jit(solution)/shard_map/psum | solution.py:34
  822.2 3.5 fusion.27
  825.8 0.0 all-reduce.23.cloned.1.call-update
  825.8 6.4 multiply_subtract_fusion
  832.1 83.9 %all-reduce.23.cloned.1.call-done = f32[128,128]{0,1:T(8,128)} async-done(((f32[128,128]{0,1:T(8,128)}), f32[128,128]{0,1:T(8,128)}) %all-reduce.23.cloned.1.call-update) | async-done | bytes 65552 | tf_op jit(solution)/shard_map/psum | solution.py:35
  916.1 0.9 copy.13
  917.0 0.9 fusion.15
  917.9 11.7 %cholesky.107 = f32[128,128]{1,0:T(8,128)S(1)} custom-call(f32[128,128]{1,0:T(8,128)S(1)} %fusion.15), custom_call_target="Cholesky" | custom-call | tf_op jit(solution)/shard_map/jit(cholesky)/cholesky | solution.py:10
  929.6 0.6 compare_reduce_fusion
  930.3 0.7 fusion.13
  930.9 9.8 %custom-call.13 = f32[1,128,128]{1,2,0:T(8,128)S(1)} custom-call(f32[1,128,128]{2,1,0:T(8,128)S(1)} %fusion.13), custom_call_target="InvertDiagBlocksLowerTriangular" | custom-call | tf_op jit(solution)/shard_map/jit(_solve_triangular)/triangular_solve | solution.py:11
  940.7 1.0 fusion
  941.7 1.2 copy.15
  (19 shorter events, 0.3 us)
Async XLA Ops:
  7.2 1.2 copy-start
  7.2 232.7 %copy-start.1 = (bf16[512,1664]{1,0:T(8,128)(2,1)S(1)}, bf16[512,1664]{1,0:T(8,128)(2,1)}, u32[]{:S(2)}) copy-start(bf16[512,1664]{1,0:T(8,128)(2,1)} %param.9) | copy-start | bytes 5111812
  7.2 104.4 %all-reduce.9.cloned.1.call-start = ((), (), s32[]{:S(2)}) async-start(), calls=%async_computation | async-start | bytes 524288 | tf_op jit(solution)/shard_map/psum | solution.py:28
  14.5 198.6 %all-reduce.11.cloned.1.call-start = ((), (), s32[]{:S(2)}) async-start(), calls=%async_computation.1 | async-start | bytes 131072 | tf_op jit(solution)/shard_map/psum | solution.py:29
  113.8 244.0 %all-reduce.13.cloned.1.call-start = ((), (), s32[]{:S(2)}) async-start(), calls=%async_computation.2 | async-start | bytes 1703936 | tf_op jit(solution)/shard_map/psum | solution.py:34
  239.1 0.7 copy-start.4
  248.2 203.3 %all-reduce.15.cloned.1.call-start = ((), (), s32[]{:S(2)}) async-start(), calls=%async_computation.3 | async-start | bytes 131072 | tf_op jit(solution)/shard_map/psum | solution.py:35
  361.4 114.8 %copy-start.2 = (f32[1664,128]{1,0:T(8,128)S(1)}, f32[1664,128]{1,0:T(8,128)}, u32[]{:S(2)}) copy-start(f32[1664,128]{1,0:T(8,128)} %all-reduce.13.cloned.1.call-done) | copy-start | bytes 2555908
  361.4 215.5 %all-reduce.17.cloned.1.call-start = ((), (), s32[]{:S(2)}) async-start(), calls=%async_computation.4 | async-start | bytes 524288 | tf_op jit(solution)/shard_map/psum | solution.py:28
  482.9 195.3 %all-reduce.19.cloned.1.call-start = ((), (), s32[]{:S(2)}) async-start(), calls=%async_computation.5 | async-start | bytes 131072 | tf_op jit(solution)/shard_map/psum | solution.py:29
  579.1 133.8 %copy-start.5 = (f32[128,512]{1,0:T(8,128)S(1)}, f32[128,512]{1,0:T(8,128)}, u32[]{:S(2)}) copy-start(f32[128,512]{1,0:T(8,128)} %copy-done.4) | copy-start | bytes 786436
  579.1 243.1 %all-reduce.21.cloned.1.call-start = ((), (), s32[]{:S(2)}) async-start(), calls=%async_computation.6 | async-start | bytes 1703936 | tf_op jit(solution)/shard_map/psum | solution.py:34
  712.7 203.4 %all-reduce.23.cloned.1.call-start = ((), (), s32[]{:S(2)}) async-start(), calls=%async_computation.7 | async-start | bytes 131072 | tf_op jit(solution)/shard_map/psum | solution.py:35
  825.8 115.0 %copy-start.3 = (f32[1664,128]{1,0:T(8,128)S(1)}, f32[1664,128]{1,0:T(8,128)}, u32[]{:S(2)}) copy-start(f32[1664,128]{1,0:T(8,128)} %all-reduce.21.cloned.1.call-done) | copy-start | bytes 2555908
Sparse Core Ops, SparseCore 0:
  14.6 96.8 all-reduce.8
  114.6 98.5 all-reduce.10
  248.3 109.3 all-reduce.12
  361.7 89.7 all-reduce.14
  483.1 93.7 all-reduce.16
  579.7 98.5 all-reduce.18
  712.8 109.3 all-reduce.20
  826.3 89.7 all-reduce.22
where the time goes:
time: 954 us; the launch traced here: 950 us
  waiting for transfers between devices  773 us (81%)
  other arithmetic  94.9 us (10%)
  matrix products  58.6 us (6%)
  between operations  14.6 us (2%)
    psum x2, waiting for transfers between devices, shards(): right_raw = lax.psum(partial_right, 'row')  218 us
    psum x2, waiting for transfers between devices, shards(): gram_left = lax.psum(gram_of(proj), 'row')  198 us
    psum x2, waiting for transfers between devices, shards(): lax.psum(jnp.dot(current, current_basis, precision=lax.Precision.HIGHEST)...  191 us
    psum x2, waiting for transfers between devices, shards(): gram_right = lax.psum(gram_of(right_raw), 'col')  166 us
    another operation x12, other arithmetic, chol_solve(): lower = jnp.linalg.cholesky(gram)  49.6 us
    another operation x8, other arithmetic, chol_solve(): return jax.scipy.linalg.solve_triangular(lower, share.T, lower=True).T  41.9 us
  transfers between devices with their start and end apart: 8, of which 8 were waited for; matrix products, arithmetic and copies ran while one was open for 2% of the time, Pallas kernels for 0%

commit v1 on v0

--- a/solution.py
+++ b/solution.py
@@ -31,7 +31,11 @@
         partial_right = lax.dot_general(
             current, left, (((0,), (0,)), ((), ())), precision=lax.Precision.HIGHEST
         )
-        right_raw = lax.psum(partial_right, "row")
+        right_raw = partial_right
+        for hop in (1, 2, 4, 8):
+            right_raw = right_raw + lax.ppermute(
+                right_raw, "row", [(dev, dev ^ hop) for dev in range(16)]
+            )
         gram_right = lax.psum(gram_of(right_raw), "col")
         basis = chol_solve(right_raw, gram_right)
         outer = lax.dot_general(

time: 954 us -> 943 us (0.988)
  waiting for transfers between devices: 773 us -> 751 us
  starting transfers between devices: 1.12 us -> 14.5 us
    psum x2 -> x0, waiting for transfers between devices: 218 us -> none  [shards(): right_raw = lax.psum(partial_right, 'row')]
    ppermute x0 -> x8, waiting for transfers between devices: none -> 197 us  [shards(): lax.ppermute(right_raw, 'row', [(dev, dev ^ hop) for dev in range(16)])]
    ppermute x0 -> x8, starting transfers between devices: none -> 13.9 us  [shards(): lax.ppermute(right_raw, 'row', [(dev, dev ^ hop) for dev in range(16)])]
  transfers between devices with their start and end apart: 8 -> 14, of which waited for: 8 -> 14; matrix products, arithmetic and copies ran while one was open for 2% -> 2% of each run, Pallas kernels for 0% -> 0%
where the time goes in v1:
time: 943 us; the launch traced here: 939 us
  waiting for transfers between devices  751 us (80%)
  other arithmetic  95.6 us (10%)
  matrix products  54.9 us (6%)
  between operations  14.6 us (2%)
  starting transfers between devices  14.5 us (2%)
    psum x2, waiting for transfers between devices, shards(): gram_left = lax.psum(gram_of(proj), 'row')  198 us
    ppermute x8, waiting for transfers between devices, shards(): lax.ppermute(right_raw, 'row', [(dev, dev ^ hop) for dev in range(16)])  197 us
    psum x2, waiting for transfers between devices, shards(): lax.psum(jnp.dot(current, current_basis, precision=lax.Precision.HIGHEST)...  191 us
    psum x2, waiting for transfers between devices, shards(): gram_right = lax.psum(gram_of(right_raw), 'col')  166 us
    another operation x12, other arithmetic, chol_solve(): lower = jnp.linalg.cholesky(gram)  49.6 us
    another operation x8, other arithmetic, chol_solve(): return jax.scipy.linalg.solve_triangular(lower, share.T, lower=True).T  41.9 us
  transfers between devices with their start and end apart: 14, of which 14 were waited for; matrix products, arithmetic and copies ran while one was open for 2% of the time, Pallas kernels for 0%

profile of v1, /device:TPU:2, one launch (start us, length us, event | category | flops | bytes accessed | tf_op | source)
XLA Modules:
  0.0 938.9 jit_solution(5570601442040502553)
XLA Ops:
  7.2 1.1 copy-done
  8.3 6.2 fusion.2
  14.6 97.0 %all-reduce.7.cloned.1.call-done = f32[512,128]{1,0:T(8,128)} async-done(((f32[512,128]{1,0:T(8,128)}), f32[512,128]{1,0:T(8,128)}) %all-reduce.7.cloned.1.call-update) | async-done | bytes 262160 | tf_op jit(solution)/shard_map/psum | solution.py:28
  111.6 2.2 fusion.30
  114.1 99.1 %all-reduce.9.cloned.1.call-done = f32[128,128]{0,1:T(8,128)} async-done(((f32[128,128]{0,1:T(8,128)}), f32[128,128]{0,1:T(8,128)}) %all-reduce.9.cloned.1.call-update) | async-done | bytes 65552 | tf_op jit(solution)/shard_map/psum | solution.py:29
  213.1 0.9 copy.7
  214.0 0.9 fusion.21
  214.9 11.7 %cholesky.74 = f32[128,128]{1,0:T(8,128)S(1)} custom-call(f32[128,128]{1,0:T(8,128)S(1)} %fusion.21), custom_call_target="Cholesky" | custom-call | tf_op jit(solution)/shard_map/jit(cholesky)/cholesky | solution.py:10
  226.6 0.6 compare_reduce_fusion.3
  227.3 0.7 fusion.10
  228.0 9.8 %custom-call.10 = f32[1,128,128]{1,2,0:T(8,128)S(1)} custom-call(f32[1,128,128]{2,1,0:T(8,128)S(1)} %fusion.10), custom_call_target="InvertDiagBlocksLowerTriangular" | custom-call | tf_op jit(solution)/shard_map/jit(_solve_triangular)/triangular_solve | solution.py:11
  237.8 1.4 fusion.8
  239.2 7.6 fusion.1
  246.8 0.9 collective-permute-start
  247.7 2.0 collective-permute-done
  249.8 2.3 collective-permute-start.1
  252.1 19.5 %collective-permute-done.1 = f32[1664,128]{1,0:T(8,128)S(1)} collective-permute-done((f32[1664,128]{1,0:T(8,128)S(1)}, f32[1664,128]{1,0:T(8,128)S(1)}, u32[]{:S(2)}, u32[]{:S(2)}) %collective-permute-start.1) | collective-permute-done | bytes 852000 | tf_op jit(solution)/shard_map/ppermute | solution.py:36
  271.6 2.1 collective-permute-start.2
  273.7 37.8 %collective-permute-done.2 = f32[1664,128]{1,0:T(8,128)S(1)} collective-permute-done((f32[1664,128]{1,0:T(8,128)S(1)}, f32[1664,128]{1,0:T(8,128)S(1)}, u32[]{:S(2)}, u32[]{:S(2)}) %collective-permute-start.2) | collective-permute-done | bytes 852000 | tf_op jit(solution)/shard_map/ppermute | solution.py:36
  311.6 1.8 collective-permute-start.3
  313.4 39.6 %collective-permute-done.3 = f32[1664,128]{1,0:T(8,128)S(1)} collective-permute-done((f32[1664,128]{1,0:T(8,128)S(1)}, f32[1664,128]{1,0:T(8,128)S(1)}, u32[]{:S(2)}, u32[]{:S(2)}) %collective-permute-start.3) | collective-permute-done | bytes 852000 | tf_op jit(solution)/shard_map/ppermute | solution.py:36
  353.0 0.9 copy-done.2
  353.9 2.1 fusion.27
  356.2 7.3 multiply_subtract_fusion.1
  363.5 82.3 %all-reduce.11.cloned.1.call-done = f32[128,128]{0,1:T(8,128)} async-done(((f32[128,128]{0,1:T(8,128)}), f32[128,128]{0,1:T(8,128)}) %all-reduce.11.cloned.1.call-update) | async-done | bytes 65552 | tf_op jit(solution)/shard_map/psum | solution.py:39
  445.8 0.9 copy.9
  446.7 0.9 fusion.19
  447.6 11.7 %cholesky.85 = f32[128,128]{1,0:T(8,128)S(1)} custom-call(f32[128,128]{1,0:T(8,128)S(1)} %fusion.19), custom_call_target="Cholesky" | custom-call | tf_op jit(solution)/shard_map/jit(cholesky)/cholesky | solution.py:10
  459.3 0.7 compare_reduce_fusion.2
  460.1 0.7 fusion.11
  460.8 9.8 %custom-call.11 = f32[1,128,128]{1,2,0:T(8,128)S(1)} custom-call(f32[1,128,128]{2,1,0:T(8,128)S(1)} %fusion.11), custom_call_target="InvertDiagBlocksLowerTriangular" | custom-call | tf_op jit(solution)/shard_map/jit(_solve_triangular)/triangular_solve | solution.py:11
  470.6 2.1 fusion.4
  472.7 5.6 fusion.31
  478.3 93.8 %all-reduce.13.cloned.1.call-done = f32[512,128]{1,0:T(8,128)} async-done(((f32[512,128]{1,0:T(8,128)}), f32[512,128]{1,0:T(8,128)}) %all-reduce.13.cloned.1.call-update) | async-done | bytes 262160 | tf_op jit(solution)/shard_map/psum | solution.py:28
  572.2 2.2 fusion.32
  574.7 98.8 %all-reduce.15.cloned.1.call-done = f32[128,128]{0,1:T(8,128)} async-done(((f32[128,128]{0,1:T(8,128)}), f32[128,128]{0,1:T(8,128)}) %all-reduce.15.cloned.1.call-update) | async-done | bytes 65552 | tf_op jit(solution)/shard_map/psum | solution.py:29
  673.5 0.9 copy.11
  674.4 0.9 fusion.17
  675.3 11.7 %cholesky.96 = f32[128,128]{1,0:T(8,128)S(1)} custom-call(f32[128,128]{1,0:T(8,128)S(1)} %fusion.17), custom_call_target="Cholesky" | custom-call | tf_op jit(solution)/shard_map/jit(cholesky)/cholesky | solution.py:10
  687.0 0.6 compare_reduce_fusion.1
  687.7 0.7 fusion.12
  688.3 9.8 %custom-call.12 = f32[1,128,128]{1,2,0:T(8,128)S(1)} custom-call(f32[1,128,128]{2,1,0:T(8,128)S(1)} %fusion.12), custom_call_target="InvertDiagBlocksLowerTriangular" | custom-call | tf_op jit(solution)/shard_map/jit(_solve_triangular)/triangular_solve | solution.py:11
  698.1 1.4 fusion.6
  699.5 7.6 fusion.33
  707.1 0.7 collective-permute-start.4
  707.8 2.0 collective-permute-done.4
  709.9 2.2 collective-permute-start.5
  712.2 19.5 %collective-permute-done.5 = f32[1664,128]{1,0:T(8,128)S(1)} collective-permute-done((f32[1664,128]{1,0:T(8,128)S(1)}, f32[1664,128]{1,0:T(8,128)S(1)}, u32[]{:S(2)}, u32[]{:S(2)}) %collective-permute-start.5) | collective-permute-done | bytes 852000 | tf_op jit(solution)/shard_map/ppermute | solution.py:36
  731.7 2.1 collective-permute-start.6
  733.8 37.8 %collective-permute-done.6 = f32[1664,128]{1,0:T(8,128)S(1)} collective-permute-done((f32[1664,128]{1,0:T(8,128)S(1)}, f32[1664,128]{1,0:T(8,128)S(1)}, u32[]{:S(2)}, u32[]{:S(2)}) %collective-permute-start.6) | collective-permute-done | bytes 852000 | tf_op jit(solution)/shard_map/ppermute | solution.py:36
  771.7 1.8 collective-permute-start.7
  773.7 1.0 copy.14
  774.7 38.5 %collective-permute-done.7 = f32[1664,128]{1,0:T(8,128)S(1)} collective-permute-done((f32[1664,128]{1,0:T(8,128)S(1)}, f32[1664,128]{1,0:T(8,128)S(1)}, u32[]{:S(2)}, u32[]{:S(2)}) %collective-permute-start.7) | collective-permute-done | bytes 852000 | tf_op jit(solution)/shard_map/ppermute | solution.py:36
  813.2 2.2 fusion.23
  815.3 6.1 multiply_subtract_fusion
  821.4 83.6 %all-reduce.17.cloned.1.call-done = f32[128,128]{0,1:T(8,128)} async-done(((f32[128,128]{0,1:T(8,128)}), f32[128,128]{0,1:T(8,128)}) %all-reduce.17.cloned.1.call-update) | async-done | bytes 65552 | tf_op jit(solution)/shard_map/psum | solution.py:39
  905.0 0.9 copy.13
  906.0 0.9 fusion.15
  906.8 11.7 %cholesky.107 = f32[128,128]{1,0:T(8,128)S(1)} custom-call(f32[128,128]{1,0:T(8,128)S(1)} %fusion.15), custom_call_target="Cholesky" | custom-call | tf_op jit(solution)/shard_map/jit(cholesky)/cholesky | solution.py:10
  918.6 0.6 compare_reduce_fusion
  919.2 0.7 fusion.13
  919.9 9.8 %custom-call.13 = f32[1,128,128]{1,2,0:T(8,128)S(1)} custom-call(f32[1,128,128]{2,1,0:T(8,128)S(1)} %fusion.13), custom_call_target="InvertDiagBlocksLowerTriangular" | custom-call | tf_op jit(solution)/shard_map/jit(_solve_triangular)/triangular_solve | solution.py:11
  929.7 1.0 fusion
  930.6 1.2 copy.15
  (33 shorter events, 1.5 us)
Async XLA Ops:
  7.2 1.2 copy-start
  7.2 232.0 %copy-start.1 = (bf16[512,1664]{1,0:T(8,128)(2,1)S(1)}, bf16[512,1664]{1,0:T(8,128)(2,1)}, u32[]{:S(2)}) copy-start(bf16[512,1664]{1,0:T(8,128)(2,1)} %param.9) | copy-start | bytes 5111812
  7.2 104.4 %all-reduce.7.cloned.1.call-start = ((), (), s32[]{:S(2)}) async-start(), calls=%async_computation | async-start | bytes 524288 | tf_op jit(solution)/shard_map/psum | solution.py:28
  14.5 198.6 %all-reduce.9.cloned.1.call-start = ((), (), s32[]{:S(2)}) async-start(), calls=%async_computation.1 | async-start | bytes 131072 | tf_op jit(solution)/shard_map/psum | solution.py:29
  113.8 332.0 %all-reduce.11.cloned.1.call-start = ((), (), s32[]{:S(2)}) async-start(), calls=%async_computation.2 | async-start | bytes 131072 | tf_op jit(solution)/shard_map/psum | solution.py:39
  239.2 10.6 %copy-start.3 = (f32[128,512]{1,0:T(8,128)}, f32[128,512]{1,0:T(8,128)S(1)}, u32[]{:S(2)}) copy-start(f32[128,512]{1,0:T(8,128)S(1)} %fusion.8) | copy-start | bytes 786436
  246.8 2.9 collective-permute-start
  249.8 21.7 %collective-permute-start.1 = (f32[1664,128]{1,0:T(8,128)S(1)}, f32[1664,128]{1,0:T(8,128)S(1)}, u32[]{:S(2)}, u32[]{:S(2)}) collective-permute-start(f32[1664,128]{1,0:T(8,128)S(1)} %add.51), channel_id=1, source_target_pairs={{0,32},{16,48},{32,0},{48,16},{64,96},{80,112},{96,64},{112,80},{1... | collective-permute-start | bytes 2555912 | tf_op jit(solution)/shard_map/ppermute | solution.py:36
  271.6 39.9 %collective-permute-start.2 = (f32[1664,128]{1,0:T(8,128)S(1)}, f32[1664,128]{1,0:T(8,128)S(1)}, u32[]{:S(2)}, u32[]{:S(2)}) collective-permute-start(f32[1664,128]{1,0:T(8,128)S(1)} %add.52), channel_id=1, source_target_pairs={{0,64},{16,80},{32,96},{48,112},{64,0},{80,16},{96,32},{112,48},{1... | collective-permute-start | bytes 2555912 | tf_op jit(solution)/shard_map/ppermute | solution.py:36
  311.6 41.4 %collective-permute-start.3 = (f32[1664,128]{1,0:T(8,128)S(1)}, f32[1664,128]{1,0:T(8,128)S(1)}, u32[]{:S(2)}, u32[]{:S(2)}) collective-permute-start(f32[1664,128]{1,0:T(8,128)S(1)} %add.53), channel_id=1, source_target_pairs={{0,128},{16,144},{32,160},{48,176},{64,192},{80,208},{96,224},{112... | collective-permute-start | bytes 2555912 | tf_op jit(solution)/shard_map/ppermute | solution.py:36
  353.0 0.9 copy-start.2
  356.1 216.1 %all-reduce.13.cloned.1.call-start = ((), (), s32[]{:S(2)}) async-start(), calls=%async_computation.3 | async-start | bytes 524288 | tf_op jit(solution)/shard_map/psum | solution.py:28
  478.3 195.2 %all-reduce.15.cloned.1.call-start = ((), (), s32[]{:S(2)}) async-start(), calls=%async_computation.4 | async-start | bytes 131072 | tf_op jit(solution)/shard_map/psum | solution.py:29
  574.4 330.6 %all-reduce.17.cloned.1.call-start = ((), (), s32[]{:S(2)}) async-start(), calls=%async_computation.5 | async-start | bytes 131072 | tf_op jit(solution)/shard_map/psum | solution.py:39
  707.1 66.5 %copy-start.4 = (f32[128,512]{1,0:T(8,128)S(1)}, f32[128,512]{1,0:T(8,128)}, u32[]{:S(2)}) copy-start(f32[128,512]{1,0:T(8,128)} %copy-done.3) | copy-start | bytes 786436
  707.1 2.7 collective-permute-start.4
  709.9 21.7 %collective-permute-start.5 = (f32[1664,128]{1,0:T(8,128)S(1)}, f32[1664,128]{1,0:T(8,128)S(1)}, u32[]{:S(2)}, u32[]{:S(2)}) collective-permute-start(f32[1664,128]{1,0:T(8,128)S(1)} %add.55), channel_id=1, source_target_pairs={{0,32},{16,48},{32,0},{48,16},{64,96},{80,112},{96,64},{112,80},{1... | collective-permute-start | bytes 2555912 | tf_op jit(solution)/shard_map/ppermute | solution.py:36
  731.7 39.9 %collective-permute-start.6 = (f32[1664,128]{1,0:T(8,128)S(1)}, f32[1664,128]{1,0:T(8,128)S(1)}, u32[]{:S(2)}, u32[]{:S(2)}) collective-permute-start(f32[1664,128]{1,0:T(8,128)S(1)} %add.56), channel_id=1, source_target_pairs={{0,64},{16,80},{32,96},{48,112},{64,0},{80,16},{96,32},{112,48},{1... | collective-permute-start | bytes 2555912 | tf_op jit(solution)/shard_map/ppermute | solution.py:36
  771.7 41.4 %collective-permute-start.7 = (f32[1664,128]{1,0:T(8,128)S(1)}, f32[1664,128]{1,0:T(8,128)S(1)}, u32[]{:S(2)}, u32[]{:S(2)}) collective-permute-start(f32[1664,128]{1,0:T(8,128)S(1)} %add.57), channel_id=1, source_target_pairs={{0,128},{16,144},{32,160},{48,176},{64,192},{80,208},{96,224},{112... | collective-permute-start | bytes 2555912 | tf_op jit(solution)/shard_map/ppermute | solution.py:36
Sparse Core Ops, SparseCore 0:
  14.6 96.8 all-reduce.6
  114.6 98.5 all-reduce.8
  356.2 89.5 all-reduce.10
  478.4 93.7 all-reduce.12
  574.9 98.5 all-reduce.14
  815.5 89.5 all-reduce.16
